TPU v7x, 32 devices: a whole 2x2x4 slice. The times are simulated.
32 devices in a mesh: group: 2 (over y), cache: 8 (over z, x), tensor: 2 (over core).
Axes of the slice: x: 2, y: 2, z: 4, core: 2. Of those that a mesh axis runs over, the one named last changes fastest.
Arguments:
- tokens: bfloat16 [2048, 8192], P(('group', 'cache'), 'tensor'), parts along dimension 0, may hold values from -6 to 6
- tenant_ids: int32 [2048, 1], P(('group', 'cache')), parts along dimension 0, may hold values from 0 to 7; in each aligned block of 128 rows (0 to 127, 128 to 255, ...) at most 32 rows name the same one
- owner_map: int32 [8], replicated, may hold values from 0 to 7, each once
- adapter_a: bfloat16 [8, 8192, 192], P('cache', 'tensor'), may hold values from -0.0625 to 0.0625
- adapter_bq: bfloat16 [8, 64, 8192], P('cache', None, 'tensor'), may hold values from -0.75 to 0.75
- adapter_bkv: bfloat16 [8, 2, 64, 1024], P('cache', None, None, 'tensor'), may hold values from -0.75 to 0.75
Outputs:
- query_delta: bfloat16 [2048, 8192], P(('group', 'cache'), 'tensor'), parts along dimension 0
- kv_delta: bfloat16 [2, 2048, 1024], P(None, ('group', 'cache'), 'tensor'), parts along dimension 1
There are 2 independent parts, one for each index of `group`. A program takes and returns all parts, laid end to end along the dimension named above; an argument that names none is the same for every part. Nothing has to cross between parts.
Inputs may be any that keep to these rules, and one draw needn't show every extreme that they name: `tenant_ids`: in the rows of one cache index (aligned blocks of 128 rows) no tenant appears more than 32 times, and some tenant appears exactly 32 times. `owner_map`: each cache index holds exactly one tenant's adapter.
All inputs are finite; a program needn't handle non-finite values.
Results may differ from a plain program's by a relative error of at most 0.005.
Values may be sent and summed in bfloat16 or wider, within the bound.
A program may use at most 64 MiB of HBM per device.

v0:
```python
import jax
import jax.numpy as jnp
from jax import lax
from jax.sharding import PartitionSpec as P


def project_low(block, local_a):
    return jnp.dot(block, local_a, preferred_element_type=jnp.float32)


def expand_low(low, query_b, kv_b, rank):
    query = jnp.dot(low[:, :rank], query_b, preferred_element_type=jnp.float32).astype(jnp.bfloat16)
    keys = jnp.dot(low[:, rank : 2 * rank], kv_b[0], preferred_element_type=jnp.float32).astype(
        jnp.bfloat16
    )
    values = jnp.dot(low[:, 2 * rank :], kv_b[1], preferred_element_type=jnp.float32).astype(
        jnp.bfloat16
    )
    return (query, jnp.concatenate([keys, values], axis=1))


def local(tokens, tenant_ids, owner_map, adapter_a, adapter_bq, adapter_bkv):
    rows, half = tokens.shape
    peers = lax.axis_size("cache")
    capacity = max(2, 2 * rows // peers)
    slots = peers * capacity
    tenants = owner_map.shape[0]
    local_a = adapter_a[0]
    query_b = adapter_bq[0]
    kv_b = adapter_bkv[0]
    rank = query_b.shape[0]
    kv_half = kv_b.shape[2]
    tenant_of = tenant_ids[:, 0]
    match = tenant_of[:, None] == jnp.arange(tenants, dtype=jnp.int32)[None, :]
    holder = jnp.sum(jnp.where(match, owner_map[None, :], 0), axis=1)
    hits = (holder[:, None] == jnp.arange(peers, dtype=jnp.int32)[None, :]).astype(jnp.int32)
    before = jnp.cumsum(hits, axis=0) - hits
    place = holder * capacity + jnp.sum(before * hits, axis=1)
    placing = (place[None, :] == jnp.arange(slots, dtype=jnp.int32)[:, None]).astype(jnp.bfloat16)
    outgoing = jnp.dot(placing, tokens, preferred_element_type=jnp.float32).astype(jnp.bfloat16)
    outgoing = outgoing.reshape(peers, capacity, half)
    block = lax.all_to_all(outgoing, "cache", split_axis=0, concat_axis=0, tiled=True)
    count = block.shape[1]
    flat = block.reshape(peers * count, half)
    low = lax.psum(project_low(flat, local_a), "tensor").astype(jnp.bfloat16)
    query, keyval = expand_low(low, query_b, kv_b, rank)
    query = query.reshape(peers, count, half)
    keyval = keyval.reshape(peers, count, 2 * kv_half)
    back_q = lax.all_to_all(query, "cache", split_axis=0, concat_axis=0, tiled=True)
    back_kv = lax.all_to_all(keyval, "cache", split_axis=0, concat_axis=0, tiled=True)
    gathering = placing.T
    query_delta = jnp.dot(
        gathering, back_q.reshape(slots, half), preferred_element_type=jnp.float32
    ).astype(jnp.bfloat16)
    keyval = jnp.dot(
        gathering, back_kv.reshape(slots, 2 * kv_half), preferred_element_type=jnp.float32
    ).astype(jnp.bfloat16)
    kv_delta = jnp.stack([keyval[:, :kv_half], keyval[:, kv_half:]], axis=0)
    return (query_delta, kv_delta)


def solution(mesh):
    in_specs = (
        P(("group", "cache"), "tensor"),
        P(("group", "cache"), None),
        P(),
        P("cache", "tensor", None),
        P("cache", None, "tensor"),
        P("cache", None, None, "tensor"),
    )
    out_specs = (P(("group", "cache"), "tensor"), P(None, ("group", "cache"), "tensor"))
    return jax.shard_map(local, mesh=mesh, in_specs=in_specs, out_specs=out_specs, check_vma=False)
```

profile of v0, /device:TPU:0, one launch (start us, length us, event | category | flops | bytes accessed | tf_op | source)
XLA Modules:
  0.0 139.6 jit_solution(13043911112348682436)
XLA Ops:
  0.6 0.0 copy-start
  0.6 1.0 select_reduce_fusion.1
  1.6 0.1 fusion.10
  1.7 0.2 reduce_window_sum.11
  1.9 0.2 select_reduce_fusion
  2.1 1.9 %convolution_convert_fusion = bf16[256,4096]{1,0:T(8,128)(2,1)S(1)} fusion(bf16[128,4096]{1,0:T(8,128)(2,1)} %param.6, s32[128]{0:T(128)S(1)} %multiply_add_fusion), kind=kOutput, calls=%fused_computation | convolution fusion | flops 269516800 | bytes 3146240 | tf_op jit(solution)/shard_map/dot_general | solution.py:40
  4.0 55.3 %all_to_all.15 = bf16[8,32,4096]{2,1,0:T(8,128)(2,1)S(1)} all-to-all(bf16[8,32,4096]{2,1,0:T(8,128)(2,1)S(1)} %bitcast.29), channel_id=1, replica_groups=mesh['group'=2,'cache'=8,'tensor'=2] {'cache'}, dimensions={0} | all-to-all | bytes 4194304 | tf_op jit(solution)/shard_map/all_to_all | solution.py:42
  59.3 0.0 copy-start.2
  59.3 0.0 copy-done
  59.3 0.8 fusion
  60.1 0.0 copy-start.1
  60.2 4.1 %all-reduce.1 = bf16[256,192]{0,1:T(8,128)(2,1)S(1)} all-reduce(f32[256,192]{0,1:T(8,128)S(1)} %fusion), channel_id=1, replica_groups=mesh['group'=2,'cache'=8,'tensor'=2] {'tensor'}, use_global_device_ids=true, to_apply=%region_3.4 | all-reduce | flops 49152 | bytes 294912 | tf_op jit(solution)/shard_map/psum | solution.py:45
  64.3 0.0 copy-done.2
  64.3 0.2 convolution_convert_fusion.3
  64.5 0.2 convolution_convert_fusion.4
  64.8 0.9 pad_maximum_fusion
  65.6 3.6 %all-to-all-start.2 = ((bf16[8,32,1024]{2,1,0:T(8,128)(2,1)}), bf16[8,32,1024]{2,1,0:T(8,128)(2,1)S(1)}, u32[]{:S(2)}, u32[]{:S(2)}) async-start(bf16[8,32,1024]{2,1,0:T(8,128)(2,1)} %bitcast.9), calls=%async_computation.2 | async-start | bytes 1048576 | tf_op jit(solution)/shard_map/all_to_all | solution.py:50
  69.3 0.0 copy-done.1
  69.3 2.0 %convolution_convert_fusion.1 = bf16[256,4096]{1,0:T(8,128)(2,1)} fusion(bf16[1,64,4096]{2,1,0:T(8,128)(2,1)S(1)} %copy-done.1, bf16[256,192]{0,1:T(8,128)(2,1)S(1)} %all-reduce.1), kind=kOutput, calls=%fused_computation.1 | convolution fusion | flops 135266304 | bytes 2654208 | tf_op jit(solution)/shard_map/dot_general | solution.py:12
  71.3 13.1 %all-to-all-done.2 = bf16[8,32,1024]{2,1,0:T(8,128)(2,1)S(1)} async-done(((bf16[8,32,1024]{2,1,0:T(8,128)(2,1)}), bf16[8,32,1024]{2,1,0:T(8,128)(2,1)S(1)}, u32[]{:S(2)}, u32[]{:S(2)}) %all-to-all-start.2) | async-done | bytes 524320 | tf_op jit(solution)/shard_map/all_to_all | solution.py:50
  84.4 4.3 %all-to-all-start.1 = ((bf16[8,32,4096]{2,1,0:T(8,128)(2,1)}), bf16[8,32,4096]{2,1,0:T(8,128)(2,1)}, u32[]{:S(2)}, u32[]{:S(2)}) async-start(bf16[8,32,4096]{2,1,0:T(8,128)(2,1)} %bitcast.27), calls=%async_computation.1 | async-start | bytes 4194304 | tf_op jit(solution)/shard_map/all_to_all | solution.py:49
  88.7 0.3 convolution_convert_fusion.5
  89.0 0.7 pad_maximum_fusion.1
  89.7 46.8 %all-to-all-done.1 = bf16[8,32,4096]{2,1,0:T(8,128)(2,1)} async-done(((bf16[8,32,4096]{2,1,0:T(8,128)(2,1)}), bf16[8,32,4096]{2,1,0:T(8,128)(2,1)}, u32[]{:S(2)}, u32[]{:S(2)}) %all-to-all-start.1) | async-done | bytes 2097184 | tf_op jit(solution)/shard_map/all_to_all | solution.py:49
  136.5 3.1 %convolution_convert_fusion.2 = bf16[128,4096]{1,0:T(8,128)(2,1)} fusion(bf16[256,4096]{1,0:T(8,128)(2,1)} %bitcast.6, s32[128]{0:T(128)S(1)} %multiply_add_fusion), kind=kOutput, calls=%fused_computation.2 | convolution fusion | flops 268992512 | bytes 3146240 | tf_op jit(solution)/shard_map/dot_general | solution.py:52
  (2 shorter events, 0.0 us)
Async XLA Ops:
  0.6 58.7 %copy-start = (bf16[1,4096,192]{1,2,0:T(8,128)(2,1)S(1)}, bf16[1,4096,192]{1,2,0:T(8,128)(2,1)}, u32[]{:S(2)}) copy-start(bf16[1,4096,192]{1,2,0:T(8,128)(2,1)} %param.9) | copy-start | bytes 4718596
  59.3 5.0 %copy-start.2 = (bf16[1,2,64,512]{3,2,1,0:T(8,128)(2,1)S(1)}, bf16[1,2,64,512]{3,2,1,0:T(8,128)(2,1)}, u32[]{:S(2)}) copy-start(bf16[1,2,64,512]{3,2,1,0:T(8,128)(2,1)} %param.11) | copy-start | bytes 393220
  60.1 9.1 %copy-start.1 = (bf16[1,64,4096]{2,1,0:T(8,128)(2,1)S(1)}, bf16[1,64,4096]{2,1,0:T(8,128)(2,1)}, u32[]{:S(2)}) copy-start(bf16[1,64,4096]{2,1,0:T(8,128)(2,1)} %param.10) | copy-start | bytes 1572868
  65.6 18.7 %all-to-all-start.2 = ((bf16[8,32,1024]{2,1,0:T(8,128)(2,1)}), bf16[8,32,1024]{2,1,0:T(8,128)(2,1)S(1)}, u32[]{:S(2)}, u32[]{:S(2)}) async-start(bf16[8,32,1024]{2,1,0:T(8,128)(2,1)} %bitcast.9), calls=%async_computation.2 | async-start | bytes 1048576 | tf_op jit(solution)/shard_map/all_to_all | solution.py:50
  84.4 52.2 %all-to-all-start.1 = ((bf16[8,32,4096]{2,1,0:T(8,128)(2,1)}), bf16[8,32,4096]{2,1,0:T(8,128)(2,1)}, u32[]{:S(2)}, u32[]{:S(2)}) async-start(bf16[8,32,4096]{2,1,0:T(8,128)(2,1)} %bitcast.27), calls=%async_computation.1 | async-start | bytes 4194304 | tf_op jit(solution)/shard_map/all_to_all | solution.py:49
where the time goes:
time: 140 us
  waiting for transfers between devices  59.9 us (43%)
  blocking collectives  59.4 us (42%)
  matrix products  8.59 us (6%)
  starting transfers between devices  7.94 us (6%)
  other arithmetic  2.99 us (2%)
    all_to_all x1, blocking collectives, local(): lax.all_to_all(outgoing, 'cache', split_axis=0, concat_axis=0, tiled=True)  55.3 us
    all_to_all x1, waiting for transfers between devices, local(): lax.all_to_all(query, 'cache', split_axis=0, concat_axis=0, tiled=True)  46.8 us
    all_to_all x1, waiting for transfers between devices, local(): lax.all_to_all(keyval, 'cache', split_axis=0, concat_axis=0, tiled=True)  13.1 us
    all_to_all x1, starting transfers between devices, local(): lax.all_to_all(query, 'cache', split_axis=0, concat_axis=0, tiled=True)  4.34 us
    psum x1, blocking collectives, local(): low = lax.psum(project_low(flat, local_a), 'tensor').astype(jnp.bfloat16)  4.1 us
    all_to_all x1, starting transfers between devices, local(): lax.all_to_all(keyval, 'cache', split_axis=0, concat_axis=0, tiled=True)  3.61 us
    dot_general x1, matrix products, local(): jnp.dot(gathering, back_q.reshape(slots, half), preferred_element_type=jn...  3.05 us
  transfers between devices with their start and end apart: 2, of which 2 were waited for; matrix products, arithmetic and copies ran while one was open for 2% of the time, Pallas kernels for 0%

commit v1 on v0

--- a/solution.py
+++ b/solution.py
@@ -17,6 +17,29 @@
         jnp.bfloat16
     )
     return (query, jnp.concatenate([keys, values], axis=1))
+
+
+GATHER_LIMIT = 8 << 20
+
+
+def expand_at_holder(low, query_b, kv_b, placing, peers, count):
+    slots, rows = placing.shape
+    rank, half = query_b.shape
+    kv_half = kv_b.shape[2]
+    query, keyval = expand_low(low, query_b, kv_b, rank)
+    query = query.reshape(peers, count, half)
+    keyval = keyval.reshape(peers, count, 2 * kv_half)
+    back_q = lax.all_to_all(query, "cache", split_axis=0, concat_axis=0, tiled=True)
+    back_kv = lax.all_to_all(keyval, "cache", split_axis=0, concat_axis=0, tiled=True)
+    gathering = placing.T
+    query_delta = jnp.dot(
+        gathering, back_q.reshape(slots, half), preferred_element_type=jnp.float32
+    ).astype(jnp.bfloat16)
+    keyval = jnp.dot(
+        gathering, back_kv.reshape(slots, 2 * kv_half), preferred_element_type=jnp.float32
+    ).astype(jnp.bfloat16)
+    kv_delta = jnp.stack([keyval[:, :kv_half], keyval[:, kv_half:]], axis=0)
+    return (query_delta, kv_delta)
 
 
 def local(tokens, tenant_ids, owner_map, adapter_a, adapter_bq, adapter_bkv):
@@ -43,20 +66,23 @@
     count = block.shape[1]
     flat = block.reshape(peers * count, half)
     low = lax.psum(project_low(flat, local_a), "tensor").astype(jnp.bfloat16)
-    query, keyval = expand_low(low, query_b, kv_b, rank)
-    query = query.reshape(peers, count, half)
-    keyval = keyval.reshape(peers, count, 2 * kv_half)
-    back_q = lax.all_to_all(query, "cache", split_axis=0, concat_axis=0, tiled=True)
-    back_kv = lax.all_to_all(keyval, "cache", split_axis=0, concat_axis=0, tiled=True)
-    gathering = placing.T
-    query_delta = jnp.dot(
-        gathering, back_q.reshape(slots, half), preferred_element_type=jnp.float32
+    if peers * (query_b.size + kv_b.size) * 2 > GATHER_LIMIT:
+        return expand_at_holder(low, query_b, kv_b, placing, peers, count)
+    everyone_q = lax.all_gather(query_b, "cache", axis=0, tiled=True)
+    everyone_kv = lax.all_gather(kv_b, "cache", axis=1, tiled=True)
+    back = lax.all_to_all(low.reshape(peers, count, 3 * rank), "cache", split_axis=0, concat_axis=0, tiled=True)
+    mine = jnp.dot(
+        placing.T, back.reshape(slots, 3 * rank), preferred_element_type=jnp.float32
     ).astype(jnp.bfloat16)
-    keyval = jnp.dot(
-        gathering, back_kv.reshape(slots, 2 * kv_half), preferred_element_type=jnp.float32
-    ).astype(jnp.bfloat16)
-    kv_delta = jnp.stack([keyval[:, :kv_half], keyval[:, kv_half:]], axis=0)
-    return (query_delta, kv_delta)
+    spread = jnp.arange(peers * rank, dtype=jnp.int32)[None, :] // rank == holder[:, None]
+
+    def expand(j, factors):
+        part = jnp.tile(mine[:, j * rank : (j + 1) * rank], (1, peers))
+        part = jnp.where(spread, part, jnp.zeros((), jnp.bfloat16))
+        return jnp.dot(part, factors, preferred_element_type=jnp.float32).astype(jnp.bfloat16)
+
+    kv_delta = jnp.stack([expand(1, everyone_kv[0]), expand(2, everyone_kv[1])], axis=0)
+    return (expand(0, everyone_q), kv_delta)
 
 
 def solution(mesh):

time: 140 us -> 155 us (1.11)
  between operations: 0.75 us -> 14.1 us
  blocking collectives: 59.4 us -> 72 us
  waiting for transfers between devices: 59.9 us -> 52.6 us
  starting transfers between devices: 7.94 us -> 3.56 us
    all_to_all x2 -> x1, waiting for transfers between devices: 59.9 us -> 10.4 us  [local(): lax.all_to_all(low.reshape(peers, count, 3 * rank), 'cache', split_axis=0...]
    all_gather x0 -> x2, waiting for transfers between devices: none -> 40.8 us  [the longest x1 40.8 us: local(): everyone_q = lax.all_gather(query_b, 'cache', axis=0, tiled=True)]
    all_to_all x1, blocking collectives: 55.3 us -> 68 us  [local(): lax.all_to_all(outgoing, 'cache', split_axis=0, concat_axis=0, tiled=True)]
    all_to_all x2 -> x1, starting transfers between devices: 7.94 us -> 3.48 us  [local(): lax.all_to_all(low.reshape(peers, count, 3 * rank), 'cache', split_axis=0...]
    dot_general x5 -> x4, matrix products: 5.82 us -> 6.82 us  [the longest x3 6.59 us: expand(): jnp.dot(part, factors, preferred_element_type=jnp.float32)]
  transfers between devices with their start and end apart: 2 -> 3, of which waited for: 2 -> 2; matrix products, arithmetic and copies ran while one was open for 2% -> 5% of each run, Pallas kernels for 0% -> 0%
where the time goes in v1:
time: 155 us
  blocking collectives  72 us (46%)
  waiting for transfers between devices  52.6 us (34%)
  between operations  14.1 us (9%)
  matrix products  9.58 us (6%)
  starting transfers between devices  3.56 us (2%)
  other arithmetic  2.16 us (1%)
    all_to_all x1, blocking collectives, local(): lax.all_to_all(outgoing, 'cache', split_axis=0, concat_axis=0, tiled=True)  68 us
    all_gather x1, waiting for transfers between devices, local(): everyone_q = lax.all_gather(query_b, 'cache', axis=0, tiled=True)  40.8 us
    all_to_all x1, waiting for transfers between devices, local(): lax.all_to_all(low.reshape(peers, count, 3 * rank), 'cache', split_axis=0...  10.4 us
    dot_general x3, matrix products, expand(): jnp.dot(part, factors, preferred_element_type=jnp.float32)  6.59 us
    psum x1, blocking collectives, local(): low = lax.psum(project_low(flat, local_a), 'tensor').astype(jnp.bfloat16)  3.97 us
    all_to_all x1, starting transfers between devices, local(): lax.all_to_all(low.reshape(peers, count, 3 * rank), 'cache', split_axis=0...  3.48 us
  transfers between devices with their start and end apart: 3, of which 2 were waited for; matrix products, arithmetic and copies ran while one was open for 5% of the time, Pallas kernels for 0%

profile of v1, /device:TPU:0, one launch (start us, length us, event | category | flops | bytes accessed | tf_op | source)
XLA Modules:
  0.0 154.9 jit_solution(2665418979414075190)
XLA Ops:
  7.2 0.0 copy-start
  7.2 0.0 all-gather.7.cloned.1.call-start
  7.2 0.7 all-gather.7.cloned.1.call-update
  7.9 0.0 all-gather.5.cloned.1.call-start
  8.0 0.7 all-gather.5.cloned.1.call-update
  8.7 0.8 select_reduce_fusion.1
  9.5 0.1 fusion.10
  9.6 0.2 reduce_window_sum.11
  9.8 0.2 select_reduce_fusion
  10.0 1.9 %convolution_convert_fusion = bf16[256,4096]{1,0:T(8,128)(2,1)S(1)} fusion(bf16[128,4096]{1,0:T(8,128)(2,1)} %param.6, s32[128]{0:T(128)S(1)} %multiply_add_fusion.1), kind=kOutput, calls=%fused_computation | convolution fusion | flops 269516800 | bytes 3146240 | tf_op jit(solution)/shard_map/dot_general | solution.py:63
  11.9 68.0 %all_to_all.10 = bf16[8,32,4096]{2,1,0:T(8,128)(2,1)S(1)} all-to-all(bf16[8,32,4096]{2,1,0:T(8,128)(2,1)S(1)} %bitcast.30), channel_id=1, replica_groups=mesh['group'=2,'cache'=8,'tensor'=2] {'cache'}, dimensions={0} | all-to-all | bytes 4194304 | tf_op jit(solution)/shard_map/all_to_all | solution.py:65
  79.9 0.0 copy-done
  79.9 0.8 fusion.1
  80.8 4.0 %all-reduce.1 = bf16[256,192]{0,1:T(8,128)(2,1)S(1)} all-reduce(f32[256,192]{0,1:T(8,128)S(1)} %fusion.1), channel_id=1, replica_groups=mesh['group'=2,'cache'=8,'tensor'=2] {'tensor'}, use_global_device_ids=true, to_apply=%region_3.4 | all-reduce | flops 49152 | bytes 294912 | tf_op jit(solution)/shard_map/psum | solution.py:68
  84.8 0.8 copy.11
  85.5 3.5 %all-to-all-start.1 = ((bf16[8,32,192]{2,1,0:T(8,128)(2,1)}), bf16[8,32,192]{2,1,0:T(8,128)(2,1)S(1)}, u32[]{:S(2)}, u32[]{:S(2)}) async-start(bf16[8,32,192]{2,1,0:T(8,128)(2,1)} %bitcast.4), calls=%async_computation.1 | async-start | bytes 262144 | tf_op jit(solution)/shard_map/all_to_all | solution.py:73
  89.0 10.4 %all-to-all-done.1 = bf16[8,32,192]{2,1,0:T(8,128)(2,1)S(1)} async-done(((bf16[8,32,192]{2,1,0:T(8,128)(2,1)}), bf16[8,32,192]{2,1,0:T(8,128)(2,1)S(1)}, u32[]{:S(2)}, u32[]{:S(2)}) %all-to-all-start.1) | async-done | bytes 98336 | tf_op jit(solution)/shard_map/all_to_all | solution.py:73
  99.5 0.2 convolution_convert_fusion.4
  99.7 0.1 compare_select_fusion.1
  99.9 0.0 all-gather.7.cloned.1.call-done
  99.9 1.3 fusion.3
  101.2 1.3 fusion.4
  102.5 0.7 pad_maximum_fusion
  103.2 40.8 %all-gather.5.cloned.1.call-done = bf16[1,512,4096]{2,1,0:T(8,128)(2,1)} async-done(((bf16[1,64,4096]{2,1,0:T(8,128)(2,1)}), bf16[1,512,4096]{2,1,0:T(8,128)(2,1)}) %all-gather.5.cloned.1.call-update) | async-done | bytes 4194320 | tf_op jit(solution)/shard_map/all_gather | solution.py:71
  144.0 4.0 %convolution_convert_fusion.1 = bf16[128,4096]{1,0:T(8,128)(2,1)} fusion(bf16[1,512,4096]{2,1,0:T(8,128)(2,1)} %all-gather.5.cloned.1.call-done, bf16[128,512]{0,1:T(8,128)(2,1)S(1)} %bitcast.31, s32[128]{0:T(128)S(1)} %select_reduce_fusion.1, s32[512]{0:T(512)S(1)} %add_select_fusion.1), kind=kOutput, calls=%fused_computation.1 | convolution fusion | flops 537526272 | bytes 5376512 | tf_op jit(solution)/shard_map/dot_general | solution.py:82
  (5 shorter events, 0.0 us)
Async XLA Ops:
  7.2 72.8 %copy-start = (bf16[1,4096,192]{1,2,0:T(8,128)(2,1)S(1)}, bf16[1,4096,192]{1,2,0:T(8,128)(2,1)}, u32[]{:S(2)}) copy-start(bf16[1,4096,192]{1,2,0:T(8,128)(2,1)} %param.9) | copy-start | bytes 4718596
  7.2 92.7 %all-gather.7.cloned.1.call-start = ((), (), s32[]{:S(2)}) async-start(), calls=%async_computation.3 | async-start | bytes 1179648 | tf_op jit(solution)/shard_map/all_gather | solution.py:72
  7.9 136.1 %all-gather.5.cloned.1.call-start = ((), (), s32[]{:S(2)}) async-start(), calls=%async_computation.2 | async-start | bytes 4718592 | tf_op jit(solution)/shard_map/all_gather | solution.py:71
  85.5 13.9 %all-to-all-start.1 = ((bf16[8,32,192]{2,1,0:T(8,128)(2,1)}), bf16[8,32,192]{2,1,0:T(8,128)(2,1)S(1)}, u32[]{:S(2)}, u32[]{:S(2)}) async-start(bf16[8,32,192]{2,1,0:T(8,128)(2,1)} %bitcast.4), calls=%async_computation.1 | async-start | bytes 262144 | tf_op jit(solution)/shard_map/all_to_all | solution.py:73
Sparse Core Ops, SparseCore 0:
  10.2 56.0 all-gather.6
  68.4 75.5 all-gather.4

commit v2 on v0

--- a/solution.py
+++ b/solution.py
@@ -1,6 +1,8 @@
 import jax
 import jax.numpy as jnp
 from jax import lax
+from jax.experimental import pallas as pl
+from jax.experimental.pallas import tpu as pltpu
 from jax.sharding import PartitionSpec as P
 
 
@@ -59,6 +61,259 @@
     return (query_delta, kv_delta)
 
 
+MESH = pl.DeviceIdType.MESH
+BF16 = jnp.bfloat16
+
+
+def fused_kernel(
+    tokens, tenant_ids, owner_map, factors_a, factors_q, factors_kv, out_q, out_kv,
+    pack, got, held, part, other, low_out, low_back,
+    tok_send, tok_recv, up_send, up_recv, down_send, down_recv, x_send, x_recv,
+    y_send, y_recv, swap_send, swap_recv, low_send, low_recv,
+):
+    group, me, core = lax.axis_index("group"), lax.axis_index("cache"), lax.axis_index("tensor")
+    peers, capacity, half = pack.shape
+    rows = tokens.shape[0]
+    slots = peers * capacity
+    rank = factors_q.shape[0]
+    kv_half = factors_kv.shape[2]
+    width = half + 2 * kv_half
+    levels = peers // 2
+    z, x = me // 2, me % 2
+
+    def remote(src, dst, send, recv, to):
+        return pltpu.make_async_remote_copy(
+            src_ref=src, dst_ref=dst, send_sem=send, recv_sem=recv, device_id=to, device_id_type=MESH
+        )
+
+    def cache_peer(index):
+        return (group, index, core)
+
+    across = (1 - group, me, core)
+    partner = (group, me, 1 - core)
+
+    barrier = pltpu.get_barrier_semaphore()
+    for k in range(1, peers):
+        pl.semaphore_signal(barrier, inc=1, device_id=cache_peer((me + k) % peers), device_id_type=MESH)
+    pl.semaphore_signal(barrier, inc=1, device_id=across, device_id_type=MESH)
+    pl.semaphore_signal(barrier, inc=1, device_id=partner, device_id_type=MESH)
+
+    for h in range(2):
+        part_rows = pl.ds(h * rank // 2, rank // 2)
+        held[me, h, :, 0:half] = factors_q[part_rows, :]
+        held[me, h, :, half : half + kv_half] = factors_kv[0, part_rows, :]
+        held[me, h, :, half + kv_half : width] = factors_kv[1, part_rows, :]
+
+    pl.semaphore_wait(barrier, peers + 1)
+
+    def factor(owner, send, recv, to):
+        return remote(held.at[owner, group], held.at[owner, group], send, recv, to)
+
+    def up(owner, d):
+        return factor(owner, up_send.at[d], up_recv.at[d], cache_peer((me + 2) % peers))
+
+    def down(owner, d):
+        return factor(owner, down_send.at[d], down_recv.at[d], cache_peer((me + peers - 2) % peers))
+
+    def sideways(owner):
+        return factor(owner, x_send.at[owner // 2], x_recv.at[owner // 2], cache_peer(z * 2 + 1 - x))
+
+    def over(owner):
+        return factor(owner, y_send.at[owner], y_recv.at[owner], across)
+
+    def over_in(owner):
+        return remote(
+            held.at[owner, 1 - group], held.at[owner, 1 - group], y_send.at[owner], y_recv.at[owner], across
+        )
+
+    pl.when(z < levels - 1)(lambda: up(me, 1).start())
+    pl.when(z > 0)(lambda: down(me, 1).start())
+    sideways(me).start()
+
+    tenant = tenant_ids[...]
+    holder = jnp.zeros((rows, 1), jnp.int32)
+    for i in range(peers):
+        holder = jnp.where(tenant == i, owner_map[i], holder)
+    hits = (holder == lax.broadcasted_iota(jnp.int32, (rows, peers), 1)).astype(jnp.float32)
+    earlier = (
+        lax.broadcasted_iota(jnp.int32, (rows, rows), 1) < lax.broadcasted_iota(jnp.int32, (rows, rows), 0)
+    ).astype(BF16)
+    before = jnp.dot(earlier, hits.astype(BF16), preferred_element_type=jnp.float32)
+    place = holder.astype(jnp.float32) * capacity + jnp.sum(before * hits, axis=1, keepdims=True)
+    gathering = (
+        place == lax.broadcasted_iota(jnp.int32, (rows, slots), 1).astype(jnp.float32)
+    ).astype(jnp.float32)
+    placing = gathering.T.astype(BF16)
+    gathering = gathering.astype(BF16)
+
+    step = min(half, 512)
+    for start in range(0, half, step):
+        cols = pl.ds(start, step)
+        pack[:, :, cols] = (
+            jnp.dot(placing, tokens[:, cols], preferred_element_type=jnp.float32)
+            .astype(BF16)
+            .reshape(peers, capacity, step)
+        )
+
+    def token_copy(k):
+        to = (me + k) % peers
+        return remote(pack.at[to], got.at[me], tok_send.at[k], tok_recv.at[k], cache_peer(to))
+
+    def token_in(k):
+        src = (me + peers - k) % peers
+        return remote(pack.at[src], got.at[src], tok_send.at[k], tok_recv.at[k], cache_peer(src))
+
+    order = sorted(range(1, peers), key=lambda k: abs(k - levels))
+    for k in order:
+        token_copy(k).start()
+    got[me] = pack[me]
+
+    for d in range(1, levels):
+        low_owner, high_owner = me - 2 * d, me + 2 * d
+
+        @pl.when(z >= d)
+        def _():
+            up(low_owner, d).wait_recv()
+            if d < levels - 1:
+                pl.when(z < levels - 1)(lambda: up(low_owner, d + 1).start())
+            sideways(low_owner).start()
+            over(low_owner).start()
+
+        @pl.when(z < levels - d)
+        def _():
+            down(high_owner, d).wait_recv()
+            if d < levels - 1:
+                pl.when(z > 0)(lambda: down(high_owner, d + 1).start())
+            sideways(high_owner).start()
+            over(high_owner).start()
+
+    for j in range(levels):
+        owner = ((z + j) % levels) * 2 + 1 - x
+        sideways(owner).wait_recv()
+        over(owner).start()
+
+    for k in order:
+        token_in(k).wait_recv()
+    part[...] = lax.dot_general(
+        got[...].reshape(slots, half), factors_a[...], (((1,), (1,)), ((), ())),
+        preferred_element_type=jnp.float32,
+    )
+    swap = remote(part, other, swap_send, swap_recv, partner)
+    swap.start()
+    swap.wait_recv()
+    low = (part[...] + other[...]).astype(BF16)
+    low_out[...] = low.reshape(peers, capacity, 3 * rank)
+
+    def low_copy(k):
+        to = (me + k) % peers
+        return remote(low_out.at[to], low_back.at[me], low_send.at[k], low_recv.at[k], cache_peer(to))
+
+    def low_in(k):
+        src = (me + peers - k) % peers
+        return remote(low_out.at[src], low_back.at[src], low_send.at[k], low_recv.at[k], cache_peer(src))
+
+    for k in order:
+        low_copy(k).start()
+    low_back[me] = low_out[me]
+
+    for k in range(1, peers):
+        over_in((me + k) % peers).wait_recv()
+    for k in order:
+        low_in(k).wait_recv()
+
+    mine = jnp.dot(
+        gathering, low_back[...].reshape(slots, 3 * rank), preferred_element_type=jnp.float32
+    ).astype(BF16)
+    wide = peers * rank
+    own = lax.broadcasted_iota(jnp.int32, (rows, wide), 1) // rank == holder
+
+    def spread(j):
+        at = lax.broadcasted_iota(jnp.int32, (3 * rank, wide), 0)
+        copies = at == lax.broadcasted_iota(jnp.int32, (3 * rank, wide), 1) % rank + j * rank
+        tiled = jnp.dot(mine, copies.astype(jnp.float32).astype(BF16), preferred_element_type=jnp.float32)
+        return jnp.where(own, tiled, 0.0).astype(BF16)
+
+    def term(left, cols):
+        return jnp.dot(
+            left, held[:, :, :, cols].reshape(wide, cols.size), preferred_element_type=jnp.float32
+        ).astype(BF16)
+
+    left = spread(0)
+    for start in range(0, half, step):
+        out_q[:, pl.ds(start, step)] = term(left, pl.ds(start, step))
+    for j in range(2):
+        out_kv[j] = term(spread(j + 1), pl.ds(half + j * kv_half, kv_half))
+
+    pl.when(z < levels - 1)(lambda: up(me, 1).wait_send())
+    pl.when(z > 0)(lambda: down(me, 1).wait_send())
+    sideways(me).wait_send()
+    for d in range(1, levels):
+        low_owner, high_owner = me - 2 * d, me + 2 * d
+
+        @pl.when(z >= d)
+        def _():
+            if d < levels - 1:
+                pl.when(z < levels - 1)(lambda: up(low_owner, d + 1).wait_send())
+            sideways(low_owner).wait_send()
+            over(low_owner).wait_send()
+
+        @pl.when(z < levels - d)
+        def _():
+            if d < levels - 1:
+                pl.when(z > 0)(lambda: down(high_owner, d + 1).wait_send())
+            sideways(high_owner).wait_send()
+            over(high_owner).wait_send()
+
+    for j in range(levels):
+        over(((z + j) % levels) * 2 + 1 - x).wait_send()
+    swap.wait_send()
+    for k in order:
+        token_copy(k).wait_send()
+        low_copy(k).wait_send()
+
+
+def fused(tokens, tenant_ids, owner_map, adapter_a, adapter_bq, adapter_bkv):
+    rows, half = tokens.shape
+    peers = lax.axis_size("cache")
+    capacity = max(2, 2 * rows // peers)
+    rank = adapter_bq.shape[1]
+    kv_half = adapter_bkv.shape[3]
+    levels = peers // 2
+    low = (peers, capacity, 3 * rank)
+    pairs = [levels, levels, levels, peers]
+    sems = [pltpu.SemaphoreType.DMA((peers,))] * 2
+    for number in pairs:
+        sems += [pltpu.SemaphoreType.DMA((number,))] * 2
+    sems += [pltpu.SemaphoreType.DMA] * 2 + [pltpu.SemaphoreType.DMA((peers,))] * 2
+    vmem = pl.BlockSpec(memory_space=pltpu.VMEM)
+    flops = 2 * rows * half * (2 * rows + 6 * rank + peers * rank)
+    return tuple(
+        pl.pallas_call(
+            fused_kernel,
+            out_shape=(
+                jax.ShapeDtypeStruct((rows, half), BF16),
+                jax.ShapeDtypeStruct((2, rows, kv_half), BF16),
+            ),
+            in_specs=[vmem, vmem, pl.BlockSpec(memory_space=pltpu.SMEM), vmem, vmem, vmem],
+            out_specs=(vmem, vmem),
+            scratch_shapes=[
+                pltpu.VMEM((peers, capacity, half), BF16),
+                pltpu.VMEM((peers, capacity, half), BF16),
+                pltpu.VMEM((peers, 2, rank // 2, half + 2 * kv_half), BF16),
+                pltpu.VMEM((peers * capacity, 3 * rank), jnp.float32),
+                pltpu.VMEM((peers * capacity, 3 * rank), jnp.float32),
+                pltpu.VMEM(low, BF16),
+                pltpu.VMEM(low, BF16),
+                *sems,
+            ],
+            compiler_params=pltpu.CompilerParams(
+                collective_id=0, has_side_effects=True, vmem_limit_bytes=40 << 20
+            ),
+            cost_estimate=pl.CostEstimate(flops=flops, bytes_accessed=8 << 20, transcendentals=0),
+        )(tokens, tenant_ids, owner_map, jnp.swapaxes(adapter_a[0], 0, 1), adapter_bq[0], adapter_bkv[0])
+    )
+
+
 def solution(mesh):
     in_specs = (
         P(("group", "cache"), "tensor"),
@@ -69,4 +324,6 @@
         P("cache", None, None, "tensor"),
     )
     out_specs = (P(("group", "cache"), "tensor"), P(None, ("group", "cache"), "tensor"))
-    return jax.shard_map(local, mesh=mesh, in_specs=in_specs, out_specs=out_specs, check_vma=False)
+    sizes = (mesh.shape["group"], mesh.shape["cache"], mesh.shape["tensor"])
+    body = fused if sizes == (2, 8, 2) else local
+    return jax.shard_map(body, mesh=mesh, in_specs=in_specs, out_specs=out_specs, check_vma=False)

time: 140 us -> 121 us (0.86)
  Pallas kernels: 0 us -> 112 us
  waiting for transfers between devices: 59.9 us -> 0 us
  blocking collectives: 59.4 us -> 0 us
  matrix products: 8.59 us -> 0 us
  starting transfers between devices: 7.94 us -> 0 us
  local copies, waits for them, and re-layouts: 0.04 us -> 7.66 us
  other arithmetic: 2.99 us -> 0 us
    pallas_call x0 -> x1, Pallas kernels: none -> 112 us  [fused(): pl.pallas_call(fused_kernel, out_shape=(jax.ShapeDtypeStruct((rows, half)...]
    all_to_all x2 -> x0, waiting for transfers between devices: 59.9 us -> none  [the longest x1 46.8 us: local(): lax.all_to_all(query, 'cache', split_axis=0, concat_axis=0, tiled=True)]
    all_to_all x1 -> x0, blocking collectives: 55.3 us -> none  [local(): lax.all_to_all(outgoing, 'cache', split_axis=0, concat_axis=0, tiled=True)]
    dot_general x7 -> x0, matrix products: 8.59 us -> none  [the longest x1 3.05 us: local(): jnp.dot(gathering, back_q.reshape(slots, half), preferred_element_type=jn...]
    all_to_all x2 -> x0, starting transfers between devices: 7.94 us -> none  [the longest x1 4.34 us: local(): lax.all_to_all(query, 'cache', split_axis=0, concat_axis=0, tiled=True)]
    unnamed x6 -> x13, local copies, waits for them, and re-layouts: 0.02 us -> 7.66 us
    psum x1 -> x0, blocking collectives: 4.1 us -> none  [local(): low = lax.psum(project_low(flat, local_a), 'tensor').astype(jnp.bfloat16)]
  transfers between devices with their start and end apart: 2 -> 0, of which waited for: 2 -> 0; matrix products, arithmetic and copies ran while one was open for 2% -> 0% of each run, Pallas kernels for 0% -> 0%
where the time goes in v2:
time: 121 us
  Pallas kernels  112 us (93%)
  local copies, waits for them, and re-layouts  7.66 us (6%)
    pallas_call x1, Pallas kernels, fused(): pl.pallas_call(fused_kernel, out_shape=(jax.ShapeDtypeStruct((rows, half)...  112 us
    unnamed x13, local copies, waits for them, and re-layouts  7.66 us

profile of v2, /device:TPU:0, one launch (start us, length us, event | category | flops | bytes accessed | tf_op | source)
XLA Modules:
  0.0 120.7 jit_solution(5985392513906073286)
XLA Ops:
  0.6 0.8 copy.8.tenant_ids
  1.4 0.0 copy-start
  1.4 1.4 %copy-done = bf16[1,4096,192]{1,2,0:T(8,128)(2,1)S(1)} copy-done((bf16[1,4096,192]{1,2,0:T(8,128)(2,1)S(1)}, bf16[1,4096,192]{1,2,0:T(8,128)(2,1)}, u32[]{:S(2)}) %copy-start) | copy-done | bytes 1572888
  2.8 0.0 copy-start.1
  2.8 1.2 %copy-done.1 = bf16[128,4096]{1,0:T(8,128)(2,1)S(1)} copy-done((bf16[128,4096]{1,0:T(8,128)(2,1)S(1)}, bf16[128,4096]{1,0:T(8,128)(2,1)}, u32[]{:S(2)}) %copy-start.1) | copy-done | bytes 1048600
  4.0 0.0 copy-start.2
  4.0 1.0 copy-done.2
  5.1 0.0 copy-start.3
  5.1 0.9 copy-done.3
  6.0 0.0 copy-start.4
  6.0 0.7 copy-done.4
  6.6 112.4 %shard_map.77 = (bf16[128,4096]{1,0:T(8,128)(2,1)S(1)}, bf16[2,128,512]{2,1,0:T(8,128)(2,1)S(1)}) custom-call(bf16[128,4096]{1,0:T(8,128)(2,1)S(1)} %copy-done.1, s32[128,1]{1,0:T(8,128)S(1)} %copy.8.tenant_ids, s32[8]{0:T(128)S(1)} %copy-done.4, bf16[192,4096]{1,0:T(8,128)(2,1)S(1)} %bitcast.5, bf16[64,4096]{1,0:T(8,128)(2,1)S(1)} %bitcast.6, ...), custom_call_target="tpu_custom_call" | custom-call | flops 1207959552 | bytes 8388608 | tf_op jit(solution)/shard_map/pallas_call | solution.py:291
  119.0 1.0 copy.11
  120.0 0.7 copy.12
Async XLA Ops:
  1.4 1.4 %copy-start = (bf16[1,4096,192]{1,2,0:T(8,128)(2,1)S(1)}, bf16[1,4096,192]{1,2,0:T(8,128)(2,1)}, u32[]{:S(2)}) copy-start(bf16[1,4096,192]{1,2,0:T(8,128)(2,1)} %param.9) | copy-start | bytes 4718596
  2.8 1.2 %copy-start.1 = (bf16[128,4096]{1,0:T(8,128)(2,1)S(1)}, bf16[128,4096]{1,0:T(8,128)(2,1)}, u32[]{:S(2)}) copy-start(bf16[128,4096]{1,0:T(8,128)(2,1)} %tokens.1) | copy-start | bytes 3145732
  4.0 1.0 copy-start.2
  5.1 0.9 copy-start.3
  6.0 0.7 copy-start.4

commit v3 on v2

--- a/solution.py
+++ b/solution.py
@@ -66,8 +66,8 @@
 
 
 def fused_kernel(
-    tokens, tenant_ids, owner_map, factors_a, factors_q, factors_kv, out_q, out_kv,
-    pack, got, held, part, other, low_out, low_back,
+    tokens_at, ids_at, owners_at, factors_at, factors_q, factors_kv, out_q, out_kv,
+    tokens, tenant_ids, owner_map, factors_a, fetch_sem, pack, got, held, part, other, low_out, low_back,
     tok_send, tok_recv, up_send, up_recv, down_send, down_recv, x_send, x_recv,
     y_send, y_recv, swap_send, swap_recv, low_send, low_recv,
 ):
@@ -77,7 +77,6 @@
     slots = peers * capacity
     rank = factors_q.shape[0]
     kv_half = factors_kv.shape[2]
-    width = half + 2 * kv_half
     levels = peers // 2
     z, x = me // 2, me % 2
 
@@ -98,11 +97,24 @@
     pl.semaphore_signal(barrier, inc=1, device_id=across, device_id_type=MESH)
     pl.semaphore_signal(barrier, inc=1, device_id=partner, device_id_type=MESH)
 
+    fetches = []
+
+    def fetch(src, dst):
+        copy = pltpu.make_async_copy(src, dst, fetch_sem.at[len(fetches)])
+        fetches.append(copy)
+        copy.start()
+        return copy
+
     for h in range(2):
         part_rows = pl.ds(h * rank // 2, rank // 2)
-        held[me, h, :, 0:half] = factors_q[part_rows, :]
-        held[me, h, :, half : half + kv_half] = factors_kv[0, part_rows, :]
-        held[me, h, :, half + kv_half : width] = factors_kv[1, part_rows, :]
+        fetch(factors_q.at[part_rows, :], held.at[me, h, :, pl.ds(0, half)])
+        for j in range(2):
+            fetch(factors_kv.at[j, part_rows, :], held.at[me, h, :, pl.ds(half + j * kv_half, kv_half)])
+    own_factors = list(fetches)
+    row_data = [fetch(ids_at, tenant_ids), fetch(owners_at, owner_map), fetch(tokens_at, tokens)]
+    late = fetch(factors_at, factors_a)
+    for copy in own_factors:
+        copy.wait()
 
     pl.semaphore_wait(barrier, peers + 1)
 
@@ -130,10 +142,12 @@
     pl.when(z > 0)(lambda: down(me, 1).start())
     sideways(me).start()
 
-    tenant = tenant_ids[...]
-    holder = jnp.zeros((rows, 1), jnp.int32)
-    for i in range(peers):
-        holder = jnp.where(tenant == i, owner_map[i], holder)
+    for copy in row_data:
+        copy.wait()
+    tenant = jnp.broadcast_to(tenant_ids[...], (rows, rows)).T[:, 0:1]
+    matched = tenant == lax.broadcasted_iota(jnp.int32, (rows, peers), 1)
+    holder = jnp.sum(jnp.where(matched, owner_map[...].astype(jnp.float32), 0.0), axis=1, keepdims=True)
+    holder = holder.astype(jnp.int32)
     hits = (holder == lax.broadcasted_iota(jnp.int32, (rows, peers), 1)).astype(jnp.float32)
     earlier = (
         lax.broadcasted_iota(jnp.int32, (rows, rows), 1) < lax.broadcasted_iota(jnp.int32, (rows, rows), 0)
@@ -164,8 +178,6 @@
         return remote(pack.at[src], got.at[src], tok_send.at[k], tok_recv.at[k], cache_peer(src))
 
     order = sorted(range(1, peers), key=lambda k: abs(k - levels))
-    for k in order:
-        token_copy(k).start()
     got[me] = pack[me]
 
     for d in range(1, levels):
@@ -187,6 +199,10 @@
             sideways(high_owner).start()
             over(high_owner).start()
 
+        if d == 2:
+            for k in order:
+                token_copy(k).start()
+
     for j in range(levels):
         owner = ((z + j) % levels) * 2 + 1 - x
         sideways(owner).wait_recv()
@@ -194,6 +210,7 @@
 
     for k in order:
         token_in(k).wait_recv()
+    late.wait()
     part[...] = lax.dot_general(
         got[...].reshape(slots, half), factors_a[...], (((1,), (1,)), ((), ())),
         preferred_element_type=jnp.float32,
@@ -294,9 +311,14 @@
                 jax.ShapeDtypeStruct((rows, half), BF16),
                 jax.ShapeDtypeStruct((2, rows, kv_half), BF16),
             ),
-            in_specs=[vmem, vmem, pl.BlockSpec(memory_space=pltpu.SMEM), vmem, vmem, vmem],
+            in_specs=[pl.BlockSpec(memory_space=pltpu.HBM)] * 6,
             out_specs=(vmem, vmem),
             scratch_shapes=[
+                pltpu.VMEM((rows, half), BF16),
+                pltpu.VMEM((1, rows), jnp.int32),
+                pltpu.VMEM((1, peers), jnp.int32),
+                pltpu.VMEM((3 * rank, half), BF16),
+                pltpu.SemaphoreType.DMA((10,)),
                 pltpu.VMEM((peers, capacity, half), BF16),
                 pltpu.VMEM((peers, capacity, half), BF16),
                 pltpu.VMEM((peers, 2, rank // 2, half + 2 * kv_half), BF16),
@@ -307,10 +329,17 @@
                 *sems,
             ],
             compiler_params=pltpu.CompilerParams(
-                collective_id=0, has_side_effects=True, vmem_limit_bytes=40 << 20
+                collective_id=0, has_side_effects=True, vmem_limit_bytes=56 << 20
             ),
             cost_estimate=pl.CostEstimate(flops=flops, bytes_accessed=8 << 20, transcendentals=0),
-        )(tokens, tenant_ids, owner_map, jnp.swapaxes(adapter_a[0], 0, 1), adapter_bq[0], adapter_bkv[0])
+        )(
+            tokens,
+            tenant_ids.reshape(1, rows),
+            owner_map.reshape(1, peers),
+            jnp.swapaxes(adapter_a[0], 0, 1),
+            adapter_bq[0],
+            adapter_bkv[0],
+        )
     )
 
 

time: 121 us -> 82.2 us (0.68)
  Pallas kernels: 112 us -> 78.4 us
  local copies, waits for them, and re-layouts: 7.66 us -> 3.04 us
    pallas_call x1, Pallas kernels: 112 us -> 78.4 us  [fused(): pl.pallas_call(fused_kernel, out_shape=(jax.ShapeDtypeStruct((rows, half)...]
    unnamed x13 -> x4, local copies, waits for them, and re-layouts: 7.66 us -> 3.04 us
where the time goes in v3:
time: 82.2 us; the launch traced here: 82.1 us
  Pallas kernels  78.4 us (95%)
  local copies, waits for them, and re-layouts  3.04 us (4%)
    pallas_call x1, Pallas kernels, fused(): pl.pallas_call(fused_kernel, out_shape=(jax.ShapeDtypeStruct((rows, half)...  78.4 us
    unnamed x4, local copies, waits for them, and re-layouts  3.04 us

profile of v3, /device:TPU:0, one launch (start us, length us, event | category | flops | bytes accessed | tf_op | source)
XLA Modules:
  0.0 82.1 jit_solution(16889896449858213463)
XLA Ops:
  0.6 78.4 %shard_map.77 = (bf16[128,4096]{1,0:T(8,128)(2,1)}, bf16[2,128,512]{2,1,0:T(8,128)(2,1)}) custom-call(bf16[128,4096]{1,0:T(8,128)(2,1)} %tokens_at.1, s32[1,128]{1,0:T(1,128)} %bitcast.10, s32[1,8]{1,0:T(1,128)} %bitcast.11, bf16[192,4096]{1,0:T(8,128)(2,1)} %bitcast.7, bf16[64,4096]{1,0:T(8,128)(2,1)} %bitcast.8, bf16[2,64,512]{2,1,0:T(8,128)(2,1)} %bitcast.9), custom_call_target="tpu_custom_call" | custom-call | flops 1207959552 | bytes 8388608 | tf_op jit(solution)/shard_map/pallas_call | solution.py:308
  79.0 0.0 copy-start
  79.0 2.3 %copy.10 = bf16[128,4096]{1,0:T(8,128)(2,1)} copy(bf16[128,4096]{1,0:T(8,128)(2,1)} %get-tuple-element.4) | data formatting | bytes 2097152
  81.3 0.0 copy-done
  81.3 0.7 copy.11
Async XLA Ops:
  79.0 2.3 %copy-start = (bf16[2,128,512]{2,1,0:T(8,128)(2,1)S(1)}, bf16[2,128,512]{2,1,0:T(8,128)(2,1)}, u32[]{:S(2)}) copy-start(bf16[2,128,512]{2,1,0:T(8,128)(2,1)} %get-tuple-element.5) | copy-start | bytes 786436

commit v4 on v3

--- a/solution.py
+++ b/solution.py
@@ -62,6 +62,7 @@
 
 
 MESH = pl.DeviceIdType.MESH
+SPLIT = 5
 BF16 = jnp.bfloat16
 
 
@@ -169,16 +170,18 @@
             .reshape(peers, capacity, step)
         )
 
+    order = sorted(range(1, peers), key=lambda k: abs(k - levels))
+    turn = {k: j + 1 for j, k in enumerate(order)}
+
     def token_copy(k):
         to = (me + k) % peers
-        return remote(pack.at[to], got.at[me], tok_send.at[k], tok_recv.at[k], cache_peer(to))
+        return remote(pack.at[to], got.at[turn[k]], tok_send.at[k], tok_recv.at[k], cache_peer(to))
 
     def token_in(k):
         src = (me + peers - k) % peers
-        return remote(pack.at[src], got.at[src], tok_send.at[k], tok_recv.at[k], cache_peer(src))
-
-    order = sorted(range(1, peers), key=lambda k: abs(k - levels))
-    got[me] = pack[me]
+        return remote(pack.at[src], got.at[turn[k]], tok_send.at[k], tok_recv.at[k], cache_peer(src))
+
+    got[0] = pack[me]
 
     for d in range(1, levels):
         low_owner, high_owner = me - 2 * d, me + 2 * d
@@ -208,30 +211,36 @@
         sideways(owner).wait_recv()
         over(owner).start()
 
-    for k in order:
-        token_in(k).wait_recv()
+    def low_copy(k):
+        to = (me + peers - k) % peers
+        return remote(low_out.at[turn[k]], low_back.at[me], low_send.at[k], low_recv.at[k], cache_peer(to))
+
+    def low_in(k):
+        src = (me + k) % peers
+        return remote(low_out.at[turn[k]], low_back.at[src], low_send.at[k], low_recv.at[k], cache_peer(src))
+
+    def swap(stage, first, last):
+        band = pl.ds(first * capacity, (last - first) * capacity)
+        return remote(part.at[band], other.at[band], swap_send.at[stage], swap_recv.at[stage], partner)
+
     late.wait()
-    part[...] = lax.dot_general(
-        got[...].reshape(slots, half), factors_a[...], (((1,), (1,)), ((), ())),
-        preferred_element_type=jnp.float32,
-    )
-    swap = remote(part, other, swap_send, swap_recv, partner)
-    swap.start()
-    swap.wait_recv()
-    low = (part[...] + other[...]).astype(BF16)
-    low_out[...] = low.reshape(peers, capacity, 3 * rank)
-
-    def low_copy(k):
-        to = (me + k) % peers
-        return remote(low_out.at[to], low_back.at[me], low_send.at[k], low_recv.at[k], cache_peer(to))
-
-    def low_in(k):
-        src = (me + peers - k) % peers
-        return remote(low_out.at[src], low_back.at[src], low_send.at[k], low_recv.at[k], cache_peer(src))
-
-    for k in order:
-        low_copy(k).start()
-    low_back[me] = low_out[me]
+    stages = ((0, SPLIT), (SPLIT, peers))
+    for stage, (first, last) in enumerate(stages):
+        arrived = order[max(first, 1) - 1 : last - 1]
+        for k in arrived:
+            token_in(k).wait_recv()
+        band = pl.ds(first * capacity, (last - first) * capacity)
+        part[band, :] = lax.dot_general(
+            got[first:last].reshape((last - first) * capacity, half), factors_a[...],
+            (((1,), (1,)), ((), ())), preferred_element_type=jnp.float32,
+        )
+        swap(stage, first, last).start()
+        swap(stage, first, last).wait_recv()
+        low = (part[band, :] + other[band, :]).astype(BF16)
+        low_out[first:last] = low.reshape(last - first, capacity, 3 * rank)
+        for k in arrived:
+            low_copy(k).start()
+    low_back[me] = low_out[0]
 
     for k in range(1, peers):
         over_in((me + k) % peers).wait_recv()
@@ -283,7 +292,8 @@
 
     for j in range(levels):
         over(((z + j) % levels) * 2 + 1 - x).wait_send()
-    swap.wait_send()
+    for stage, (first, last) in enumerate(stages):
+        swap(stage, first, last).wait_send()
     for k in order:
         token_copy(k).wait_send()
         low_copy(k).wait_send()
@@ -301,15 +311,15 @@
     sems = [pltpu.SemaphoreType.DMA((peers,))] * 2
     for number in pairs:
         sems += [pltpu.SemaphoreType.DMA((number,))] * 2
-    sems += [pltpu.SemaphoreType.DMA] * 2 + [pltpu.SemaphoreType.DMA((peers,))] * 2
+    sems += [pltpu.SemaphoreType.DMA((2,))] * 2 + [pltpu.SemaphoreType.DMA((peers,))] * 2
     vmem = pl.BlockSpec(memory_space=pltpu.VMEM)
     flops = 2 * rows * half * (2 * rows + 6 * rank + peers * rank)
     return tuple(
         pl.pallas_call(
             fused_kernel,
             out_shape=(
-                jax.ShapeDtypeStruct((rows, half), BF16),
-                jax.ShapeDtypeStruct((2, rows, kv_half), BF16),
+                pltpu.VMEM((rows, half), BF16),
+                pltpu.VMEM((2, rows, kv_half), BF16),
             ),
             in_specs=[pl.BlockSpec(memory_space=pltpu.HBM)] * 6,
             out_specs=(vmem, vmem),

time: 82.2 us -> 78.9 us (0.960)
  Pallas kernels: 78.4 us -> 75.7 us
  local copies, waits for them, and re-layouts: 3.04 us -> 1.67 us
    pallas_call x1, Pallas kernels: 78.4 us -> 75.7 us  [fused(): pl.pallas_call(fused_kernel, out_shape=(pltpu.VMEM((rows, half), BF16), p...]
    unnamed x4 -> x2, local copies, waits for them, and re-layouts: 3.04 us -> 1.67 us
where the time goes in v4:
time: 78.9 us; the launch traced here: 78 us
  Pallas kernels  75.7 us (96%)
  local copies, waits for them, and re-layouts  1.67 us (2%)
    pallas_call x1, Pallas kernels, fused(): pl.pallas_call(fused_kernel, out_shape=(pltpu.VMEM((rows, half), BF16), p...  75.7 us
    unnamed x2, local copies, waits for them, and re-layouts  1.67 us

profile of v4, /device:TPU:0, one launch (start us, length us, event | category | flops | bytes accessed | tf_op | source)
XLA Modules:
  0.0 78.0 jit_solution(7988684019475683083)
XLA Ops:
  0.6 75.7 %shard_map.77 = (bf16[128,4096]{1,0:T(8,128)(2,1)S(1)}, bf16[2,128,512]{2,1,0:T(8,128)(2,1)S(1)}) custom-call(bf16[128,4096]{1,0:T(8,128)(2,1)} %tokens_at.1, s32[1,128]{1,0:T(1,128)} %bitcast.10, s32[1,8]{1,0:T(1,128)} %bitcast.11, bf16[192,4096]{1,0:T(8,128)(2,1)} %bitcast.7, bf16[64,4096]{1,0:T(8,128)(2,1)} %bitcast.8, bf16[2,64,512]{2,1,0:T(8,128)(2,1)} %bitcast.9), custom_call_target="tpu_custom_call" | custom-call | flops 1207959552 | bytes 8388608 | tf_op jit(solution)/shard_map/pallas_call | solution.py:318
  76.4 1.0 %copy.10 = bf16[128,4096]{1,0:T(8,128)(2,1)} copy(bf16[128,4096]{1,0:T(8,128)(2,1)S(1)} %get-tuple-element.2) | data formatting | bytes 2097152
  77.3 0.7 copy.11

commit v5 on v4

--- a/solution.py
+++ b/solution.py
@@ -68,7 +68,7 @@
 
 def fused_kernel(
     tokens_at, ids_at, owners_at, factors_at, factors_q, factors_kv, out_q, out_kv,
-    tokens, tenant_ids, owner_map, factors_a, fetch_sem, pack, got, held, part, other, low_out, low_back,
+    tokens, tenant_ids, owner_map, factors_a, fetch_sem, copies, own, pack, got, held, part, other, low_out, low_back,
     tok_send, tok_recv, up_send, up_recv, down_send, down_recv, x_send, x_recv,
     y_send, y_recv, swap_send, swap_recv, low_send, low_recv,
 ):
@@ -182,6 +182,14 @@
         return remote(pack.at[src], got.at[turn[k]], tok_send.at[k], tok_recv.at[k], cache_peer(src))
 
     got[0] = pack[me]
+    wide = peers * rank
+    own[...] = (lax.broadcasted_iota(jnp.int32, (rows, wide), 1) // rank == holder).astype(jnp.float32)
+    for j in range(3):
+        same = (
+            lax.broadcasted_iota(jnp.int32, (3 * rank, wide), 0)
+            == lax.broadcasted_iota(jnp.int32, (3 * rank, wide), 1) % rank + j * rank
+        )
+        copies[j] = same.astype(jnp.float32).astype(BF16)
 
     for d in range(1, levels):
         low_owner, high_owner = me - 2 * d, me + 2 * d
@@ -250,14 +258,9 @@
     mine = jnp.dot(
         gathering, low_back[...].reshape(slots, 3 * rank), preferred_element_type=jnp.float32
     ).astype(BF16)
-    wide = peers * rank
-    own = lax.broadcasted_iota(jnp.int32, (rows, wide), 1) // rank == holder
-
     def spread(j):
-        at = lax.broadcasted_iota(jnp.int32, (3 * rank, wide), 0)
-        copies = at == lax.broadcasted_iota(jnp.int32, (3 * rank, wide), 1) % rank + j * rank
-        tiled = jnp.dot(mine, copies.astype(jnp.float32).astype(BF16), preferred_element_type=jnp.float32)
-        return jnp.where(own, tiled, 0.0).astype(BF16)
+        tiled = jnp.dot(mine, copies[j], preferred_element_type=jnp.float32)
+        return jnp.where(own[...] > 0.0, tiled, 0.0).astype(BF16)
 
     def term(left, cols):
         return jnp.dot(
@@ -329,6 +332,8 @@
                 pltpu.VMEM((1, peers), jnp.int32),
                 pltpu.VMEM((3 * rank, half), BF16),
                 pltpu.SemaphoreType.DMA((10,)),
+                pltpu.VMEM((3, 3 * rank, peers * rank), BF16),
+                pltpu.VMEM((rows, peers * rank), jnp.float32),
                 pltpu.VMEM((peers, capacity, half), BF16),
                 pltpu.VMEM((peers, capacity, half), BF16),
                 pltpu.VMEM((peers, 2, rank // 2, half + 2 * kv_half), BF16),

time: 78.9 us -> 78.9 us (level)
  no operation moved by 1% of the time
where the time goes in v5:
time: 78.9 us; the launch traced here: 78 us
  Pallas kernels  75.7 us (96%)
  local copies, waits for them, and re-layouts  1.67 us (2%)
    pallas_call x1, Pallas kernels, fused(): pl.pallas_call(fused_kernel, out_shape=(pltpu.VMEM((rows, half), BF16), p...  75.7 us
    unnamed x2, local copies, waits for them, and re-layouts  1.67 us

profile of v5, /device:TPU:0, one launch (start us, length us, event | category | flops | bytes accessed | tf_op | source)
XLA Modules:
  0.0 78.0 jit_solution(16344064385329935649)
XLA Ops:
  0.6 75.7 %shard_map.77 = (bf16[128,4096]{1,0:T(8,128)(2,1)S(1)}, bf16[2,128,512]{2,1,0:T(8,128)(2,1)S(1)}) custom-call(bf16[128,4096]{1,0:T(8,128)(2,1)} %tokens_at.1, s32[1,128]{1,0:T(1,128)} %bitcast.10, s32[1,8]{1,0:T(1,128)} %bitcast.11, bf16[192,4096]{1,0:T(8,128)(2,1)} %bitcast.7, bf16[64,4096]{1,0:T(8,128)(2,1)} %bitcast.8, bf16[2,64,512]{2,1,0:T(8,128)(2,1)} %bitcast.9), custom_call_target="tpu_custom_call" | custom-call | flops 1207959552 | bytes 8388608 | tf_op jit(solution)/shard_map/pallas_call | solution.py:321
  76.4 1.0 %copy.10 = bf16[128,4096]{1,0:T(8,128)(2,1)} copy(bf16[128,4096]{1,0:T(8,128)(2,1)S(1)} %get-tuple-element.2) | data formatting | bytes 2097152
  77.3 0.7 copy.11
